TPU v7x, 32 devices: a whole 2x2x4 slice. The times are simulated.
32 devices in a mesh: dp: 8 (over y, x, core), seq: 4 (over z).
Axes of the slice: x: 2, y: 2, z: 4, core: 2. Of those that a mesh axis runs over, the one named last changes fastest.
Arguments:
- inputs: bfloat16 [32768, 768], P(('dp', 'seq')), may hold values from -6 to 6
- attn_gain: bfloat16 [768], P('dp'), may hold values from 0.25 to 1.75
- qkv_weight: bfloat16 [768, 2304], P('dp'), may hold values from -0.25 to 0.25
- proj_weight: bfloat16 [768, 768], P('dp'), may hold values from -0.4375 to 0.4375
- mlp_gain: bfloat16 [768], P('dp'), may hold values from 0.25 to 1.75
- in_weight: bfloat16 [768, 2304], P('dp'), may hold values from -0.21875 to 0.21875
- out_weight: bfloat16 [1152, 768], P('dp'), may hold values from -0.25 to 0.25
- cotangent: bfloat16 [32768, 768], P(('dp', 'seq')), may hold values from -12 to 12
Outputs:
- output: bfloat16 [32768, 768], P(('dp', 'seq'))
- input_grad: bfloat16 [32768, 768], P(('dp', 'seq'))
- attn_gain_grad: float32 [768], P('dp')
- qkv_weight_grad: float32 [768, 2304], P('dp')
- proj_weight_grad: float32 [768, 768], P('dp')
- mlp_gain_grad: float32 [768], P('dp')
- in_weight_grad: float32 [768, 2304], P('dp')
- out_weight_grad: float32 [1152, 768], P('dp')
All inputs are finite; a program needn't handle non-finite values.
Results may differ from a plain program's by a relative error of at most 0.02.
Values may be sent and summed in bfloat16 or wider, within the bound.
A program may use at most 128 MiB of HBM per device.

v0:
```python
import jax
import jax.numpy as jnp
from jax import lax
from jax.sharding import PartitionSpec as P

D = 768
HEADS = 12
HEAD_DIM = 64
FF = 1152
WINDOW = 64
QBLOCK = 512


epsilon = 1e-05
theta_base = 10000.0
masked_score = -1e30


def layer_norm(features, gain_vector):
    center = features - jnp.mean(features, -1, keepdims=True)
    spread = jnp.mean(center * center, -1, keepdims=True)
    return center * lax.rsqrt(spread + epsilon) * gain_vector


def rotary_tables(positions, head_width):
    half_width = head_width // 2
    inverse_freq = theta_base ** (-(jnp.arange(half_width, dtype=jnp.float32) * 2.0) / head_width)
    angles = positions[:, None] * inverse_freq[None, :]
    cosine_table = jnp.concatenate([jnp.cos(angles), jnp.cos(angles)], -1)
    sine_table = jnp.concatenate([jnp.sin(angles), jnp.sin(angles)], -1)
    return (cosine_table[:, None, :], sine_table[:, None, :])


def rotate(features, cosine_table, sine_table):
    half_width = features.shape[-1] // 2
    turned = jnp.concatenate([-features[..., half_width:], features[..., :half_width]], -1)
    return features * cosine_table + turned * sine_table


def gated_gelu(up_values):
    gelu_input = up_values[:, :FF]
    gate_half = up_values[:, FF:]
    return jax.nn.gelu(gelu_input, approximate=False) * gate_half


def band_scores(query_block, key_block, first_row, seq_total):
    score_scale = query_block.shape[-1] ** (-0.5)
    key_span = key_block.shape[0]
    scores = (
        jnp.einsum("qhd,khd->hqk", query_block, key_block, preferred_element_type=jnp.float32)
        * score_scale
    )
    query_pos = first_row + jnp.arange(QBLOCK, dtype=jnp.int32)[:, None]
    key_pos = first_row - WINDOW + jnp.arange(key_span, dtype=jnp.int32)[None, :]
    in_band = (jnp.abs(query_pos - key_pos) <= WINDOW) & (key_pos >= 0) & (key_pos < seq_total)
    return jnp.where(in_band[None], scores, masked_score)


def band_forward(queries, key_pad, value_pad, offset, seq_total):
    row_count = queries.shape[0]
    key_span = QBLOCK + 2 * WINDOW

    def one_block(block_index):
        row_start = block_index * QBLOCK
        query_block = lax.dynamic_slice_in_dim(queries, row_start, QBLOCK, 0)
        key_block = lax.dynamic_slice_in_dim(key_pad, row_start, key_span, 0)
        value_block = lax.dynamic_slice_in_dim(value_pad, row_start, key_span, 0)
        scores = band_scores(query_block, key_block, offset + row_start, seq_total)
        row_max = jnp.max(scores, -1, keepdims=True)
        weights = jnp.exp(scores - row_max)
        row_sum = jnp.sum(weights, -1, keepdims=True)
        softmax_low = (weights / row_sum).astype(jnp.bfloat16)
        result = jnp.einsum(
            "hqk,khd->qhd", softmax_low, value_block, preferred_element_type=jnp.float32
        )
        log_sum = jnp.transpose((row_max + jnp.log(row_sum))[:, :, 0])
        return (result, log_sum)

    results, log_sums = lax.map(one_block, jnp.arange(row_count // QBLOCK, dtype=jnp.int32))
    return (results.reshape(queries.shape), log_sums.reshape(row_count, queries.shape[1]))


def band_backward(queries, key_pad, value_pad, grad_out, log_sums, offset, seq_total):
    row_count = queries.shape[0]
    key_span = QBLOCK + 2 * WINDOW
    score_scale = queries.shape[-1] ** (-0.5)

    def one_block(carried, block_index):
        key_grads, value_grads = carried
        row_start = block_index * QBLOCK
        query_block = lax.dynamic_slice_in_dim(queries, row_start, QBLOCK, 0)
        key_block = lax.dynamic_slice_in_dim(key_pad, row_start, key_span, 0)
        value_block = lax.dynamic_slice_in_dim(value_pad, row_start, key_span, 0)
        grad_block = lax.dynamic_slice_in_dim(grad_out, row_start, QBLOCK, 0)
        lse_block = lax.dynamic_slice_in_dim(log_sums, row_start, QBLOCK, 0)
        scores = band_scores(query_block, key_block, offset + row_start, seq_total)
        softmax_out = jnp.exp(scores - jnp.transpose(lse_block)[:, :, None])
        grad_probs = jnp.einsum(
            "qhd,khd->hqk", grad_block, value_block, preferred_element_type=jnp.float32
        )
        inner_sum = jnp.sum(softmax_out * grad_probs, -1, keepdims=True)
        grad_scores = (softmax_out * (grad_probs - inner_sum)).astype(jnp.bfloat16)
        query_grad = (
            jnp.einsum("hqk,khd->qhd", grad_scores, key_block, preferred_element_type=jnp.float32)
            * score_scale
        )
        key_part = (
            jnp.einsum("hqk,qhd->khd", grad_scores, query_block, preferred_element_type=jnp.float32)
            * score_scale
        )
        value_part = jnp.einsum(
            "hqk,qhd->khd",
            softmax_out.astype(jnp.bfloat16),
            grad_block,
            preferred_element_type=jnp.float32,
        )
        key_grads = lax.dynamic_update_slice_in_dim(
            key_grads,
            lax.dynamic_slice_in_dim(key_grads, row_start, key_span, 0) + key_part,
            row_start,
            0,
        )
        value_grads = lax.dynamic_update_slice_in_dim(
            value_grads,
            lax.dynamic_slice_in_dim(value_grads, row_start, key_span, 0) + value_part,
            row_start,
            0,
        )
        return ((key_grads, value_grads), query_grad)

    padded_zero = jnp.zeros(key_pad.shape, jnp.float32)
    carried, query_grads = lax.scan(
        one_block, (padded_zero, padded_zero), jnp.arange(row_count // QBLOCK, dtype=jnp.int32)
    )
    return (query_grads.reshape(queries.shape), carried[0], carried[1])


def shards(inputs, attn_gain, qkv_weight, proj_weight, mlp_gain, in_weight, out_weight, cotangent):
    gathered = (
        lax.all_gather(qkv_weight, "dp", axis=0, tiled=True),
        lax.all_gather(proj_weight, "dp", axis=0, tiled=True),
        lax.all_gather(in_weight, "dp", axis=0, tiled=True),
        lax.all_gather(out_weight, "dp", axis=0, tiled=True),
        lax.all_gather(attn_gain, "dp", axis=0, tiled=True),
        lax.all_gather(mlp_gain, "dp", axis=0, tiled=True),
    )
    qkv_full, proj_full, in_full, out_full, attn_full, mlp_full = gathered
    tokens = inputs.shape[0]
    seq_count = lax.axis_size("seq")
    seq_total = tokens * seq_count
    offset = lax.axis_index("seq") * tokens
    local_heads = HEADS // seq_count
    residual = inputs.astype(jnp.float32)
    normed_one, norm_one_back = jax.vjp(layer_norm, residual, attn_full.astype(jnp.float32))
    normed_low = normed_one.astype(jnp.bfloat16)
    projected = jnp.dot(normed_low, qkv_full, preferred_element_type=jnp.float32)
    positions = (offset + jnp.arange(tokens, dtype=jnp.int32)).astype(jnp.float32)
    cosine_table, sine_table = rotary_tables(positions, HEAD_DIM)

    def turn_pair(raw_pairs):
        return rotate(raw_pairs.reshape(tokens, 2 * HEADS, HEAD_DIM), cosine_table, sine_table)

    turned, turn_back = jax.vjp(turn_pair, projected[:, : 2 * D])
    query_low = turned[:, :HEADS].reshape(tokens, D).astype(jnp.bfloat16)
    key_low = turned[:, HEADS:].reshape(tokens, D).astype(jnp.bfloat16)
    value_low = projected[:, 2 * D :].astype(jnp.bfloat16)
    stacked = jnp.stack([query_low, key_low, value_low], 1)
    by_heads = lax.all_to_all(stacked, "seq", split_axis=2, concat_axis=0, tiled=True)
    head_queries = by_heads[:, 0].reshape(seq_total, local_heads, HEAD_DIM)
    keys_padded = jnp.pad(
        by_heads[:, 1].reshape(seq_total, local_heads, HEAD_DIM), ((WINDOW, WINDOW), (0, 0), (0, 0))
    )
    values_padded = jnp.pad(
        by_heads[:, 2].reshape(seq_total, local_heads, HEAD_DIM), ((WINDOW, WINDOW), (0, 0), (0, 0))
    )
    attended, log_sums = band_forward(head_queries, keys_padded, values_padded, 0, seq_total)
    attended_low = attended.astype(jnp.bfloat16).reshape(seq_total, D // seq_count)
    mixed_low = lax.all_to_all(attended_low, "seq", split_axis=0, concat_axis=1, tiled=True)
    attn_out = jnp.dot(mixed_low, proj_full, preferred_element_type=jnp.float32)
    hidden_state = residual + attn_out
    normed_two, norm_two_back = jax.vjp(layer_norm, hidden_state, mlp_full.astype(jnp.float32))
    normed_two_low = normed_two.astype(jnp.bfloat16)
    up_values = jnp.dot(normed_two_low, in_full, preferred_element_type=jnp.float32)
    gated, gated_back = jax.vjp(gated_gelu, up_values)
    gated_low = gated.astype(jnp.bfloat16)
    result = hidden_state + jnp.dot(gated_low, out_full, preferred_element_type=jnp.float32)
    output = result.astype(jnp.bfloat16)
    grad_result = cotangent.astype(jnp.float32)
    out_grad = jnp.einsum("tf,td->fd", gated_low, cotangent, preferred_element_type=jnp.float32)
    gated_grad = jnp.einsum("td,fd->tf", cotangent, out_full, preferred_element_type=jnp.float32)
    up_grad = gated_back(gated_grad)[0]
    up_low = up_grad.astype(jnp.bfloat16)
    in_grad = jnp.einsum("td,tf->df", normed_two_low, up_low, preferred_element_type=jnp.float32)
    normed_two_grad = jnp.einsum("tf,df->td", up_low, in_full, preferred_element_type=jnp.float32)
    hidden_part, mlp_gain_grad = norm_two_back(normed_two_grad)
    hidden_grad = grad_result + hidden_part
    attn_low = hidden_grad.astype(jnp.bfloat16)
    proj_grad = jnp.einsum("te,td->ed", mixed_low, attn_low, preferred_element_type=jnp.float32)
    mixed_grad = jnp.einsum(
        "td,ed->te", attn_low, proj_full, preferred_element_type=jnp.float32
    ).astype(jnp.bfloat16)
    grad_heads = lax.all_to_all(mixed_grad, "seq", split_axis=1, concat_axis=0, tiled=True)
    grad_heads = grad_heads.reshape(seq_total, local_heads, HEAD_DIM)
    query_grad, key_pad_grad, value_pad_grad = band_backward(
        head_queries, keys_padded, values_padded, grad_heads, log_sums, 0, seq_total
    )
    head_grads = jnp.stack(
        [
            query_grad.reshape(seq_total, D // seq_count),
            key_pad_grad[WINDOW : WINDOW + seq_total].reshape(seq_total, D // seq_count),
            value_pad_grad[WINDOW : WINDOW + seq_total].reshape(seq_total, D // seq_count),
        ],
        1,
    ).astype(jnp.bfloat16)
    token_grads = lax.all_to_all(head_grads, "seq", split_axis=0, concat_axis=2, tiled=True)
    rotated_grad = jnp.concatenate(
        [
            token_grads[:, 0].reshape(tokens, HEADS, HEAD_DIM),
            token_grads[:, 1].reshape(tokens, HEADS, HEAD_DIM),
        ],
        1,
    ).astype(jnp.float32)
    raw_grad = turn_back(rotated_grad)[0]
    proj_in_grad = jnp.concatenate([raw_grad, token_grads[:, 2].astype(jnp.float32)], 1).astype(
        jnp.bfloat16
    )
    qkv_grad = jnp.einsum("td,tf->df", normed_low, proj_in_grad, preferred_element_type=jnp.float32)
    normed_grad = jnp.einsum(
        "tf,df->td", proj_in_grad, qkv_full, preferred_element_type=jnp.float32
    )
    input_part, attn_gain_grad = norm_one_back(normed_grad)
    input_grad = (hidden_grad + input_part).astype(jnp.bfloat16)
    shares = (
        lax.psum_scatter(qkv_grad, "dp", scatter_dimension=0, tiled=True),
        lax.psum_scatter(proj_grad, "dp", scatter_dimension=0, tiled=True),
        lax.psum_scatter(in_grad, "dp", scatter_dimension=0, tiled=True),
        lax.psum_scatter(out_grad, "dp", scatter_dimension=0, tiled=True),
        lax.psum_scatter(attn_gain_grad, "dp", scatter_dimension=0, tiled=True),
        lax.psum_scatter(mlp_gain_grad, "dp", scatter_dimension=0, tiled=True),
    )
    totals = (
        lax.psum(shares[0].astype(jnp.bfloat16), "seq").astype(jnp.float32),
        lax.psum(shares[1].astype(jnp.bfloat16), "seq").astype(jnp.float32),
        lax.psum(shares[2].astype(jnp.bfloat16), "seq").astype(jnp.float32),
        lax.psum(shares[3].astype(jnp.bfloat16), "seq").astype(jnp.float32),
        lax.psum(shares[4].astype(jnp.bfloat16), "seq").astype(jnp.float32),
        lax.psum(shares[5].astype(jnp.bfloat16), "seq").astype(jnp.float32),
    )
    return (output, input_grad, totals[4], totals[0], totals[1], totals[5], totals[2], totals[3])


def solution(mesh):
    in_specs = (
        P(("dp", "seq"), None),
        P("dp"),
        P("dp", None),
        P("dp", None),
        P("dp"),
        P("dp", None),
        P("dp", None),
        P(("dp", "seq"), None),
    )
    out_specs = (
        P(("dp", "seq"), None),
        P(("dp", "seq"), None),
        P("dp"),
        P("dp", None),
        P("dp", None),
        P("dp"),
        P("dp", None),
        P("dp", None),
    )
    return jax.shard_map(shards, mesh=mesh, in_specs=in_specs, out_specs=out_specs, check_vma=False)
```

profile of v0, /device:TPU:0, one launch (start us, length us, event | category | flops | bytes accessed | tf_op | source)
XLA Modules:
  0.0 997.3 jit_solution(2272519886768296588)
XLA Ops:
  11.6 15.3 %all-reduce.11 = (bf16[768]{0:T(1024)(128)(2,1)S(1)}, bf16[768]{0:T(1024)(128)(2,1)S(1)}) all-reduce(bf16[768]{0:T(1024)(128)(2,1)S(1)} %dynamic-update-slice, bf16[768]{0:T(1024)(128)(2,1)S(1)} %dynamic-update-slice.1), channel_id=1, replica_groups=mesh['dp'=8,'seq'=4] {'dp'}, use_global_device_ids=true, to_apply=%add.6 | all-reduce | flops 1536 | bytes 6144
  29.0 17.7 %all-gather.5.cloned.1.call-done = bf16[768,2304]{1,0:T(8,128)(2,1)} async-done(((bf16[96,2304]{1,0:T(8,128)(2,1)}), bf16[768,2304]{1,0:T(8,128)(2,1)}) %all-gather.5.cloned.1.call-update) | async-done | bytes 3538960 | tf_op jit(solution)/shard_map/all_gather | solution.py:140
  46.7 6.2 fusion.81
  56.7 6.6 copy.55
  80.8 11.1 %copy.58 = bf16[1024,3,768]{0,1,2:T(4,128)(2,1)} copy(bf16[1024,3,768]{2,0,1:T(8,128)(2,1)} %pad_maximum_fusion) | data formatting | bytes 9437184 | tf_op jit(solution)/shard_map/stack | solution.py:167
  98.6 137.3 %all-to-all-done = bf16[1024,3,768]{0,1,2:T(4,128)(2,1)} async-done(((bf16[1024,3,768]{0,1,2:T(4,128)(2,1)}), bf16[1024,3,768]{0,1,2:T(4,128)(2,1)}, u32[]{:S(2)}, u32[]{:S(2)}) %all-to-all-start) | async-done | bytes 4718624 | tf_op jit(solution)/shard_map/all_to_all | solution.py:168
  246.6 67.9 %while.30 = (s32[]{:T(128)}, bf16[8,512,3,64]{1,3,2,0:T(8,128)(2,1)}, f32[8,512,3]{1,2,0:T(4,128)}, s32[8]{0:T(128)S(1)}, bf16[4224,3,64]{0,2,1:T(8,128)(2,1)}, ...) while((s32[]{:T(128)}, ...), condition=%wide.region_5.6_spmd, body=%wide.region_2.5_spmd.sunk | while | flops 265094656 | bytes 14252788 | solution.py:79
  332.6 33.3 %all-to-all-done.1 = bf16[4,1024,192]{1,2,0:T(8,128)(2,1)} async-done(((bf16[4,1024,192]{1,2,0:T(8,128)(2,1)}), bf16[4,1024,192]{1,2,0:T(8,128)(2,1)}, u32[]{:S(2)}, u32[]{:S(2)}) %all-to-all-start.1) | async-done | bytes 1572896 | tf_op jit(solution)/shard_map/all_to_all | solution.py:178
  371.3 10.7 %fusion.89 = f32[1024,2304]{1,0:T(8,128)} fusion(bf16[768,2304]{1,0:T(8,128)(2,1)} %all-gather.9.cloned.1.call-done, f32[1024,768]{0,1:T(8,128)} %copy-done.6, f32[768]{0:T(1024)S(1)} %convert_element_type.148, f32[1024]{0:T(1024)S(1)} %fusion.84, f32[1024]{0:T(1024)S(1)} %broadcast_multiply_fusion), kind=kOutput, calls=%fused_computation.152 | convolution fusion | flops 3627024384 | bytes 16133120 | tf_op jit(solution)/shard_map/dot_general | solution.py:183
  382.0 14.9 %fusion.76 = (f32[1024,1152]{1,0:T(8,128)}, f32[1024,1152]{1,0:T(8,128)S(1)}, f32[1024,1152]{1,0:T(8,128)S(1)}) fusion(f32[1024,2304]{1,0:T(8,128)} %fusion.89, bf16[1024,768]{1,0:T(8,128)(2,1)S(1)} %copy-done.15, bf16[1152,768]{1,0:T(8,128)(2,1)} %all-gather.11.cloned.1.call-done), kind=kOutput, calls=%fused_computation.125 | convolution fusion | flops 1888616448 | bytes 22216704 | tf_op jit(solution)/shard_map/td,fd->tf/dot_general | solution.py:190
  400.4 9.0 multiply_reduce_fusion.1
  432.0 11.4 %fusion.77 = f32[768,2304]{1,0:T(8,128)} fusion(f32[1024,1152]{1,0:T(8,128)} %copy-done.9, f32[1024,1152]{1,0:T(8,128)} %get-tuple-element.312, f32[1024,768]{0,1:T(8,128)} %copy-done.6, f32[768]{0:T(1024)S(1)} %convert_element_type.148, f32[1024]{0:T(1024)S(1)} %fusion.84, f32[1024]{0:T(1024)S(1)} %broadcast_multiply_fusion), kind=kOutput, calls=%fused_computation.126 | convolution fusion | flops 3631742976 | bytes 19672064 | tf_op jit(solution)/shard_map/td,tf->df/dot_general | solution.py:193
  443.5 24.9 %all-to-all-done.2 = bf16[1024,4,192]{0,2,1:T(8,128)(2,1)S(1)} async-done(((bf16[1024,4,192]{0,2,1:T(8,128)(2,1)}), bf16[1024,4,192]{0,2,1:T(8,128)(2,1)S(1)}, u32[]{:S(2)}, u32[]{:S(2)}) %all-to-all-start.2) | async-done | bytes 1572896 | tf_op jit(solution)/shard_map/all_to_all | solution.py:202
  479.1 134.9 %while.31 = (s32[]{:T(128)}, f32[4224,3,64]{0,2,1:T(8,128)}, f32[4224,3,64]{0,2,1:T(8,128)}, bf16[8,512,3,64]{1,3,2,0:T(8,128)(2,1)}, s32[8]{0:T(128)S(1)}, /*in...) while((s32[]{:T(128)}, f32[4224,3,64]{0,2,1:T(8,128)}, ...), condition=%wide.region_12.13_spmd, body=%wide.region_10.12_spmd.sunk | while | flops 640099840 | bytes 49803588 | solution.py:132
  624.4 12.8 %copy.67 = bf16[4096,3,192]{2,1,0:T(4,128)(2,1)} copy(bf16[4096,3,192]{0,2,1:T(8,128)(2,1)} %pad_maximum_fusion.1) | data formatting | bytes 9437184 | tf_op jit(solution)/shard_map/stack | solution.py:207
  637.2 190.6 %all_to_all.68 = bf16[4096,3,192]{2,1,0:T(4,128)(2,1)} all-to-all(bf16[4096,3,192]{2,1,0:T(4,128)(2,1)} %copy.67), channel_id=1, replica_groups=mesh['dp'=8,'seq'=4] {'seq'}, dimensions={0} | all-to-all | bytes 9437184 | tf_op jit(solution)/shard_map/all_to_all | solution.py:215
  827.8 12.8 %copy.69 = bf16[1024,3,4,192]{0,3,2,1:T(8,128)(2,1)} copy(bf16[1024,3,4,192]{3,1,0,2:T(4,128)(2,1)} %bitcast.117) | data formatting | bytes 9437184 | tf_op jit(solution)/shard_map/all_to_all | solution.py:215
  848.8 7.7 fusion.72
  857.2 6.7 add_convert_fusion.2
  870.4 8.6 fusion.71
  881.4 38.9 %reduce-scatter.5.cloned.1.call-done = f32[96,2304]{1,0:T(8,128)} async-done(((f32[768,2304]{1,0:T(8,128)}), f32[96,2304]{1,0:T(8,128)}) %reduce-scatter.5.cloned.1.call-update) | async-done | bytes 884752 | tf_op jit(solution)/shard_map/reduce_scatter | solution.py:234
  925.6 13.4 %all-reduce.10 = (bf16[768]{0:T(1024)(128)(2,1)S(1)}, bf16[768]{0:T(1024)(128)(2,1)S(1)}) all-reduce(f32[768]{0:T(1024)S(1)} %get-tuple-element.264, f32[768]{0:T(1024)S(1)} %get-tuple-element.262), channel_id=2, replica_groups=mesh['dp'=8,'seq'=4] {'dp'}, use_global_device_ids=true, to_apply=%region_16.17.clone | all-reduce | flops 1536 | bytes 9216
  939.1 12.3 %all-reduce.12 = (bf16[96]{0:T(256)(128)(2,1)S(1)}, bf16[96]{0:T(256)(128)(2,1)S(1)}) all-reduce(bf16[96]{0:T(256)(128)(2,1)S(1)} %dynamic-slice.9, bf16[96]{0:T(256)(128)(2,1)S(1)} %dynamic-slice.8), channel_id=1, replica_groups=mesh['dp'=8,'seq'=4] {'seq'}, use_global_device_ids=true, to_apply=%region_17.18 | all-reduce | flops 192 | bytes 768 | tf_op jit(solution)/shard_map/psum | solution.py:246
  960.5 23.2 %all-reduce.16.cloned.1.call-done = (bf16[96,2304]{1,0:T(8,128)(2,1)}, bf16[96,768]{1,0:T(8,128)(2,1)}, bf16[96,2304]{1,0:T(8,128)(2,1)}, bf16[144,768]{1,0:T(8,128)(2,1)}) async-done(((bf16[96,2304]{1,0:T(8,128)(2,1)}, bf16[96,768]{1,0:T(8,128)(2,1)}, bf16[96,2304]{1,0:T(8,128)(2,1)}, bf16[144,768]{1,0:T(8,128)(2,1)}), (bf16[96,2304]{1,0:T(8,128)(2,1)}, bf16[96,768]{1,0:T(8,128)(2,1)}, ...) | async-done | bytes 1253392 | tf_op jit(solution)/shard_map/psum | solution.py:242
  (355 shorter events, 345.3 us)
Async XLA Ops:
  7.2 39.5 %all-gather.5.cloned.1.call-start = ((), (), s32[]{:S(2)}) async-start(), calls=%async_computation.8 | async-start | bytes 3981312 | tf_op jit(solution)/shard_map/all_gather | solution.py:140
  9.7 356.2 %copy-start.1 = (bf16[1024,768]{0,1:T(8,128)(2,1)}, bf16[1024,768]{0,1:T(8,128)(2,1)S(1)}, u32[]{:S(2)}) copy-start(bf16[1024,768]{0,1:T(8,128)(2,1)S(1)} %copy.54) | copy-start | bytes 4718596
  26.9 26.0 %copy-start.21 = (f32[768]{0:T(1024)}, f32[768]{0:T(1024)S(1)}, u32[]{:S(2)}) copy-start(f32[768]{0:T(1024)S(1)} %convert_element_type.141) | copy-start | bytes 9220
  28.2 38.7 %copy-start.11 = (f32[1024,64]{0,1:T(8,128)}, f32[1024,64]{0,1:T(8,128)S(1)}, u32[]{:S(2)}) copy-start(f32[1024,64]{0,1:T(8,128)S(1)} %get-tuple-element.346) | copy-start | bytes 786436
  28.5 24.4 %copy-start.19 = (f32[1024]{0:T(1024)}, f32[1024]{0:T(1024)S(1)}, u32[]{:S(2)}) copy-start(f32[1024]{0:T(1024)S(1)} %broadcast_multiply_fusion.1) | copy-start | bytes 12292
  29.0 23.9 %copy-start.25 = (f32[1024]{0:T(1024)}, f32[1024]{0:T(1024)S(1)}, u32[]{:S(2)}) copy-start(f32[1024]{0:T(1024)S(1)} %fusion.70) | copy-start | bytes 12292
  29.0 23.9 %copy-start.23 = (f32[1024]{0:T(1024)}, f32[1024]{0:T(1024)S(1)}, u32[]{:S(2)}) copy-start(f32[1024]{0:T(1024)S(1)} %fusion.83) | copy-start | bytes 12292
  91.9 144.1 %all-to-all-start = ((bf16[1024,3,768]{0,1,2:T(4,128)(2,1)}), bf16[1024,3,768]{0,1,2:T(4,128)(2,1)}, u32[]{:S(2)}, u32[]{:S(2)}) async-start(bf16[1024,3,768]{0,1,2:T(4,128)(2,1)} %copy.58), calls=%async_computation | async-start | bytes 12582912 | tf_op jit(solution)/shard_map/all_to_all | solution.py:168
  97.1 235.5 %all-gather.7.cloned.1.call-start = ((), (), s32[]{:S(2)}) async-start(), calls=%async_computation.9 | async-start | bytes 1327104 | tf_op jit(solution)/shard_map/all_gather | solution.py:141
  97.9 273.4 %all-gather.9.cloned.1.call-start = ((), (), s32[]{:S(2)}) async-start(), calls=%async_computation.10 | async-start | bytes 3981312 | tf_op jit(solution)/shard_map/all_gather | solution.py:142
  324.6 41.3 %all-to-all-start.1 = ((bf16[4,1024,192]{1,2,0:T(8,128)(2,1)}), bf16[4,1024,192]{1,2,0:T(8,128)(2,1)}, u32[]{:S(2)}, u32[]{:S(2)}) async-start(bf16[4,1024,192]{1,2,0:T(8,128)(2,1)} %copy.62), calls=%async_computation.1 | async-start | bytes 3145728 | tf_op jit(solution)/shard_map/all_to_all | solution.py:178
  329.0 53.1 %all-gather.11.cloned.1.call-start = ((), (), s32[]{:S(2)}) async-start(), calls=%async_computation.11 | async-start | bytes 1990656 | tf_op jit(solution)/shard_map/all_gather | solution.py:143
  329.5 537.4 %reduce-scatter.7.cloned.1.call-start = ((), (), s32[]{:S(2)}) async-start(), calls=%async_computation.13 | async-start | bytes 2654208 | tf_op jit(solution)/shard_map/reduce_scatter | solution.py:235
  371.3 10.8 %copy-start.15 = (bf16[1024,768]{1,0:T(8,128)(2,1)S(1)}, bf16[1024,768]{1,0:T(8,128)(2,1)}, u32[]{:S(2)}) copy-start(bf16[1024,768]{1,0:T(8,128)(2,1)} %param.19) | copy-start | bytes 4718596
  382.0 14.9 %copy-start.8 = (f32[1024,2304]{1,0:T(8,128)S(1)}, f32[1024,2304]{1,0:T(8,128)}, u32[]{:S(2)}) copy-start(f32[1024,2304]{1,0:T(8,128)} %fusion.89) | copy-start | bytes 28311556
  400.4 9.0 copy-start.9
  417.3 451.3 %reduce-scatter.11.cloned.1.call-start = ((), (), s32[]{:S(2)}) async-start(), calls=%async_computation.15 | async-start | bytes 3981312 | tf_op jit(solution)/shard_map/reduce_scatter | solution.py:237
  428.4 40.0 %all-to-all-start.2 = ((bf16[1024,4,192]{0,2,1:T(8,128)(2,1)}), bf16[1024,4,192]{0,2,1:T(8,128)(2,1)S(1)}, u32[]{:S(2)}, u32[]{:S(2)}) async-start(bf16[1024,4,192]{0,2,1:T(8,128)(2,1)} %bitcast.135), calls=%async_computation.2 | async-start | bytes 3145728 | tf_op jit(solution)/shard_map/all_to_all | solution.py:202
  431.9 447.2 %reduce-scatter.9.cloned.1.call-start = ((), (), s32[]{:S(2)}) async-start(), calls=%async_computation.14 | async-start | bytes 7962624 | tf_op jit(solution)/shard_map/reduce_scatter | solution.py:236
  443.4 476.9 %reduce-scatter.5.cloned.1.call-start = ((), (), s32[]{:S(2)}) async-start(), calls=%async_computation.12 | async-start | bytes 7962624 | tf_op jit(solution)/shard_map/reduce_scatter | solution.py:234
  856.5 127.2 %all-reduce.16.cloned.1.call-start = ((), (), s32[]{:S(2)}) async-start(), calls=%async_computation.16 | async-start | bytes 2506752 | tf_op jit(solution)/shard_map/psum | solution.py:242
  870.4 8.6 copy-start.26
  922.3 30.1 %copy-start.5 = (bf16[1024,768]{0,1:T(8,128)(2,1)S(1)}, bf16[1024,768]{0,1:T(8,128)(2,1)}, u32[]{:S(2)}) copy-start(bf16[1024,768]{0,1:T(8,128)(2,1)} %copy.64) | copy-start | bytes 4718596
  983.8 5.7 copy-start.18
  (27 other events, 86.4 us)
Sparse Core Ops, SparseCore 0:
  9.9 36.7 all-gather.4
  99.8 24.4 all-gather.6
  126.3 33.9 all-gather.8
  331.4 26.9 all-gather.10
  417.5 40.6 reduce-scatter.6
  461.8 48.0 reduce-scatter.10
  513.9 65.5 reduce-scatter.8
  856.7 63.5 reduce-scatter.4
  923.7 59.9 all-reduce.15
where the time goes:
time: 1010 us; the launch traced here: 997 us
  waiting for transfers between devices  278 us (28%)
  matrix products  244 us (24%)
  blocking collectives  232 us (23%)
  local copies, waits for them, and re-layouts  131 us (13%)
  other arithmetic  72 us (7%)
  between operations  16.2 us (2%)
  starting transfers between devices  14.1 us (1%)
  loops' own time  10.6 us (1%)
    all_to_all x1, blocking collectives, shards(): lax.all_to_all(head_grads, 'seq', split_axis=0, concat_axis=2, tiled=True)  191 us
    all_to_all x1, waiting for transfers between devices, shards(): lax.all_to_all(stacked, 'seq', split_axis=2, concat_axis=0, tiled=True)  137 us
    dot_general x16, matrix products, band_scores(): jnp.einsum('qhd,khd->hqk', query_block, key_block, preferred_element_type...  48.2 us
    reduce_scatter x1, waiting for transfers between devices, shards(): lax.psum_scatter(qkv_grad, 'dp', scatter_dimension=0, tiled=True)  38.9 us
    all_to_all x1, waiting for transfers between devices, shards(): lax.all_to_all(attended_low, 'seq', split_axis=0, concat_axis=1, tiled=True)  33.3 us
    unnamed x2, blocking collectives  28.7 us
    dot_general x8, matrix products, one_block(): jnp.einsum('qhd,khd->hqk', grad_block, value_block, preferred_element_typ...  28.3 us
    dot_general x8, matrix products, one_block(): jnp.einsum('hqk,khd->qhd', softmax_low, value_block, preferred_element_ty...  25.1 us
  transfers between devices with their start and end apart: 12, of which 6 were waited for; matrix products, arithmetic and copies ran while one was open for 35% of the time, Pallas kernels for 0%

commit v1 on v0

v1 whole, which is shorter than its diff:
```python
import jax
import jax.numpy as jnp
from jax import lax
from jax.experimental import pallas as pl
from jax.experimental.pallas import tpu as pltpu
from jax.sharding import PartitionSpec as P

D = 768
HEADS = 12
HEAD_DIM = 64
FF = 1152
WINDOW = 64
BLOCK = 128
SPAN = BLOCK + 2 * WINDOW
PAIR = 2 * HEAD_DIM

epsilon = 1e-05
theta_base = 10000.0
masked_score = -1e30
bf16, f32 = jnp.bfloat16, jnp.float32


def norm_parts(features):
    center = features - jnp.mean(features, -1, keepdims=True)
    spread = jnp.mean(center * center, -1, keepdims=True)
    scale = lax.rsqrt(spread + epsilon)
    return center * scale, scale


def norm_back(grad, xhat, scale):
    return scale * (
        grad - jnp.mean(grad, -1, keepdims=True) - xhat * jnp.mean(grad * xhat, -1, keepdims=True)
    )


def rotary_tables(positions):
    half = HEAD_DIM // 2
    inverse_freq = theta_base ** (-(jnp.arange(half, dtype=f32) * 2.0) / HEAD_DIM)
    angles = positions[:, None] * inverse_freq[None, :]
    cosine, sine = jnp.cos(angles), jnp.sin(angles)
    return (
        jnp.concatenate([cosine, cosine, cosine, cosine], -1),
        jnp.concatenate([-sine, sine, -sine, sine], -1),
    )


def turn(values):
    lane = lax.broadcasted_iota(jnp.int32, values.shape, 1)
    low_half = (lane & (HEAD_DIM - 1)) < HEAD_DIM // 2
    return jnp.where(
        low_half,
        pltpu.roll(values, PAIR - HEAD_DIM // 2, 1),
        pltpu.roll(values, HEAD_DIM // 2, 1),
    )


def split_heads(pair):
    lane = lax.broadcasted_iota(jnp.int32, pair.shape, 1)
    zero = jnp.zeros_like(pair)
    first = jnp.where(lane < HEAD_DIM, pair, zero)
    second = jnp.where(lane < HEAD_DIM, zero, pair)
    return jnp.concatenate([first, second], 0).astype(bf16)


def join_heads(stacked):
    lane = lax.broadcasted_iota(jnp.int32, (BLOCK, PAIR), 1)
    return jnp.where(lane < HEAD_DIM, stacked[:BLOCK], stacked[BLOCK:])


def dot_last(left, right):
    return lax.dot_general(left, right, (((1,), (1,)), ((), ())), preferred_element_type=f32)


def dot_first(left, right):
    return lax.dot_general(left, right, (((0,), (0,)), ((), ())), preferred_element_type=f32)


def attention_kernel(
    edge_ref, q_ref, k_ref, v_ref, cos_ref, sin_ref, o_ref, p_ref, qo_ref, ko_ref, vo_ref
):
    blocks = o_ref.shape[0] // BLOCK
    for start in range(0, k_ref.shape[0], BLOCK):
        rows = pl.ds(start, BLOCK)
        raw = k_ref[rows, :]
        ko_ref[rows, :] = (raw * cos_ref[rows, :] + turn(raw) * sin_ref[rows, :]).astype(bf16)
        vo_ref[rows, :] = v_ref[rows, :].astype(bf16)
    row = lax.broadcasted_iota(jnp.int32, (2 * BLOCK, SPAN), 0) & (BLOCK - 1)
    column = lax.broadcasted_iota(jnp.int32, (2 * BLOCK, SPAN), 1)
    band = (column >= row) & (column - row <= 2 * WINDOW)
    for index in range(blocks):
        own = pl.ds(index * BLOCK, BLOCK)
        wide = pl.ds(index * BLOCK + WINDOW, BLOCK)
        keys = pl.ds(index * BLOCK, SPAN)
        raw = q_ref[wide, :]
        query = (raw * cos_ref[wide, :] + turn(raw) * sin_ref[wide, :]).astype(bf16)
        qo_ref[own, :] = query
        scores = dot_last(split_heads(query.astype(f32) * HEAD_DIM**-0.5), ko_ref[keys, :])
        valid = band
        if index == 0:
            valid = valid & (column >= edge_ref[0])
        if index == blocks - 1:
            valid = valid & (column < edge_ref[1])
        scores = jnp.where(valid, scores, masked_score)
        weights = jnp.exp(scores - jnp.max(scores, -1, keepdims=True))
        probs = (weights * (1.0 / jnp.sum(weights, -1, keepdims=True))).astype(bf16)
        p_ref[0, index] = probs
        mixed = jnp.dot(probs, vo_ref[keys, :], preferred_element_type=f32)
        o_ref[own, :] = join_heads(mixed).astype(bf16)


def attention_back_kernel(
    do_ref, q_ref, k_ref, v_ref, p_ref, cos_ref, sin_ref, dq_ref, dk_ref, dv_ref
):
    blocks = do_ref.shape[0] // BLOCK
    scale = HEAD_DIM**-0.5

    def turn_back(grad, rows):
        return (grad * cos_ref[rows, :] - turn(grad) * sin_ref[rows, :]).astype(bf16)

    dk_carry = dv_carry = jnp.zeros((BLOCK, PAIR), f32)
    for index in range(blocks):
        own = pl.ds(index * BLOCK, BLOCK)
        wide = pl.ds(index * BLOCK + WINDOW, BLOCK)
        keys = pl.ds(index * BLOCK, SPAN)
        grad = split_heads(do_ref[own, :].astype(f32))
        query = split_heads(q_ref[own, :].astype(f32) * scale)
        low = p_ref[0, index]
        probs = low.astype(f32)
        grad_probs = dot_last(grad, v_ref[keys, :])
        inner = jnp.sum(probs * grad_probs, -1, keepdims=True)
        grad_scores = (probs * (grad_probs - inner)).astype(bf16)
        dq = join_heads(jnp.dot(grad_scores, k_ref[keys, :], preferred_element_type=f32)) * scale
        dq_ref[own, :] = turn_back(dq, wide)
        dk_part = dot_first(grad_scores, query)
        dv_part = dot_first(low, grad)
        dk_ref[own, :] = turn_back(dk_carry + dk_part[:BLOCK], own)
        dv_ref[own, :] = (dv_carry + dv_part[:BLOCK]).astype(bf16)
        dk_carry, dv_carry = dk_part[BLOCK:], dv_part[BLOCK:]
    last = pl.ds(blocks * BLOCK, BLOCK)
    dk_ref[last, :] = turn_back(dk_carry, last)
    dv_ref[last, :] = dv_carry.astype(bf16)


def column_spec(rows, first=0):
    return pl.BlockSpec((rows, PAIR), lambda pair: (0, pair + first))


def attention(edges, projected, cosine, sine):
    wide = projected.shape[0]
    tokens = wide - 2 * WINDOW
    pairs = HEADS // 2
    blocks = tokens // BLOCK
    table = pl.BlockSpec((wide, PAIR), lambda pair: (0, 0))
    return pl.pallas_call(
        attention_kernel,
        grid=(pairs,),
        in_specs=[
            pl.BlockSpec(memory_space=pltpu.SMEM),
            column_spec(wide),
            column_spec(wide, pairs),
            column_spec(wide, 2 * pairs),
            table,
            table,
        ],
        out_specs=[
            column_spec(tokens),
            pl.BlockSpec((1, blocks, 2 * BLOCK, SPAN), lambda pair: (pair, 0, 0, 0)),
            column_spec(tokens),
            column_spec(wide),
            column_spec(wide),
        ],
        out_shape=[
            jax.ShapeDtypeStruct((tokens, D), bf16),
            jax.ShapeDtypeStruct((pairs, blocks, 2 * BLOCK, SPAN), bf16),
            jax.ShapeDtypeStruct((tokens, D), bf16),
            jax.ShapeDtypeStruct((wide, D), bf16),
            jax.ShapeDtypeStruct((wide, D), bf16),
        ],
        cost_estimate=pl.CostEstimate(
            flops=4 * D * tokens * SPAN, bytes_accessed=30_000_000, transcendentals=HEADS * tokens * SPAN
        ),
        compiler_params=pltpu.CompilerParams(vmem_limit_bytes=40 * 1024 * 1024),
        name="attention_forward",
    )(edges, projected, projected, projected, cosine, sine)


def attention_back(grad_mixed, query, key, value, probs, cosine, sine):
    wide = key.shape[0]
    tokens = wide - 2 * WINDOW
    pairs = HEADS // 2
    blocks = tokens // BLOCK
    table = pl.BlockSpec((wide, PAIR), lambda pair: (0, 0))
    return pl.pallas_call(
        attention_back_kernel,
        grid=(pairs,),
        in_specs=[
            column_spec(tokens),
            column_spec(tokens),
            column_spec(wide),
            column_spec(wide),
            pl.BlockSpec((1, blocks, 2 * BLOCK, SPAN), lambda pair: (pair, 0, 0, 0)),
            table,
            table,
        ],
        out_specs=[column_spec(tokens), column_spec(wide), column_spec(wide)],
        out_shape=[
            jax.ShapeDtypeStruct((tokens, D), bf16),
            jax.ShapeDtypeStruct((wide, D), bf16),
            jax.ShapeDtypeStruct((wide, D), bf16),
        ],
        cost_estimate=pl.CostEstimate(
            flops=8 * D * tokens * SPAN, bytes_accessed=20_000_000, transcendentals=0
        ),
        compiler_params=pltpu.CompilerParams(vmem_limit_bytes=40 * 1024 * 1024),
        name="attention_backward",
    )(grad_mixed, query, key, value, probs, cosine, sine)


def gather(weight):
    return lax.all_gather(weight, "dp", axis=0, tiled=True)


def scatter_sum(grad):
    share = lax.psum_scatter(grad.astype(bf16), "dp", scatter_dimension=0, tiled=True)
    return lax.psum(share, "seq").astype(f32)


def shards(inputs, attn_gain, qkv_weight, proj_weight, mlp_gain, in_weight, out_weight, cotangent):
    tokens = inputs.shape[0]
    seq_count = lax.axis_size("seq")
    place = lax.axis_index("seq")
    forward = [(i, i + 1) for i in range(seq_count - 1)]
    backward = [(i + 1, i) for i in range(seq_count - 1)]

    qkv_full = gather(qkv_weight)
    attn_full = gather(attn_gain).astype(f32)
    mlp_full = gather(mlp_gain).astype(f32)
    proj_full = gather(proj_weight)
    in_full = gather(in_weight)
    out_full = gather(out_weight)

    before = lax.ppermute(inputs[-WINDOW:], "seq", forward)
    after = lax.ppermute(inputs[:WINDOW], "seq", backward)
    x_wide = jnp.concatenate([before, inputs, after], 0).astype(f32)
    xhat_wide, scale_wide = norm_parts(x_wide)
    n1_wide = (xhat_wide * attn_full).astype(bf16)
    projected = jnp.dot(n1_wide, qkv_full, preferred_element_type=f32)
    positions = (place * tokens - WINDOW + jnp.arange(tokens + 2 * WINDOW, dtype=jnp.int32)).astype(
        f32
    )
    cosine, sine = rotary_tables(positions)
    edges = jnp.stack(
        [jnp.where(place == 0, WINDOW, 0), jnp.where(place == seq_count - 1, SPAN - WINDOW, SPAN)]
    ).astype(jnp.int32)
    mixed, probs, query, key, value = attention(edges, projected, cosine, sine)

    residual = inputs.astype(f32)
    hidden = residual + jnp.dot(mixed, proj_full, preferred_element_type=f32)
    xhat_two, scale_two = norm_parts(hidden)
    n2 = (xhat_two * mlp_full).astype(bf16)
    up = jnp.dot(n2, in_full, preferred_element_type=f32)
    a, g = up[:, :FF], up[:, FF:]
    cdf = 0.5 * (1.0 + lax.erf(a * (0.5**0.5)))
    gelu = a * cdf
    gelu_slope = cdf + a * (jnp.exp(-0.5 * a * a) * (0.5 / jnp.pi) ** 0.5)
    m = (gelu * g).astype(bf16)
    output = (hidden + jnp.dot(m, out_full, preferred_element_type=f32)).astype(bf16)

    out_grad = jnp.einsum("tf,td->fd", m, cotangent, preferred_element_type=f32)
    out_total = scatter_sum(out_grad)
    dm = jnp.einsum("td,fd->tf", cotangent, out_full, preferred_element_type=f32)
    du = jnp.concatenate([dm * g * gelu_slope, dm * gelu], 1).astype(bf16)
    in_grad = jnp.einsum("td,tf->df", n2, du, preferred_element_type=f32)
    in_total = scatter_sum(in_grad)
    dn2 = jnp.einsum("tf,df->td", du, in_full, preferred_element_type=f32)
    dh = cotangent.astype(f32) + norm_back(dn2 * mlp_full, xhat_two, scale_two)
    da = dh.astype(bf16)
    proj_grad = jnp.einsum("te,td->ed", mixed, da, preferred_element_type=f32)
    proj_total = scatter_sum(proj_grad)
    grad_mixed = jnp.einsum("td,ed->te", da, proj_full, preferred_element_type=f32).astype(bf16)

    dq, dk_wide, dv_wide = attention_back(grad_mixed, query, key, value, probs, cosine, sine)
    own = slice(WINDOW, WINDOW + tokens)
    kv_head = jnp.concatenate([dk_wide[:WINDOW], dv_wide[:WINDOW]], 1)
    kv_tail = jnp.concatenate([dk_wide[-WINDOW:], dv_wide[-WINDOW:]], 1)
    from_after = lax.ppermute(kv_head, "seq", backward)
    from_before = lax.ppermute(kv_tail, "seq", forward)
    qkv_grad = jnp.concatenate(
        [
            dot_first(n1_wide[own], dq).astype(bf16),
            dot_first(n1_wide, dk_wide).astype(bf16),
            dot_first(n1_wide, dv_wide).astype(bf16),
        ],
        1,
    )
    qkv_total = scatter_sum(qkv_grad)
    kv = jnp.concatenate([dk_wide[own], dv_wide[own]], 1)
    kv = jnp.concatenate(
        [
            (kv[:WINDOW].astype(f32) + from_before.astype(f32)).astype(bf16),
            kv[WINDOW:-WINDOW],
            (kv[-WINDOW:].astype(f32) + from_after.astype(f32)).astype(bf16),
        ],
        0,
    )
    dproj = jnp.concatenate([dq, kv], 1)
    dn1 = dot_last(dproj, qkv_full)
    xhat_one, scale_one = norm_parts(residual)
    input_grad = (dh + norm_back(dn1 * attn_full, xhat_one, scale_one)).astype(bf16)

    attn_gain_grad = jnp.sum(qkv_weight.astype(f32) * qkv_total, -1) / attn_gain.astype(f32)
    mlp_gain_grad = jnp.sum(in_weight.astype(f32) * in_total, -1) / mlp_gain.astype(f32)
    return (
        output,
        input_grad,
        attn_gain_grad,
        qkv_total,
        proj_total,
        mlp_gain_grad,
        in_total,
        out_total,
    )


def solution(mesh):
    rows, split = P(("dp", "seq"), None), P("dp", None)
    in_specs = (rows, P("dp"), split, split, P("dp"), split, split, rows)
    out_specs = (rows, rows, P("dp"), split, split, P("dp"), split, split)
    return jax.shard_map(shards, mesh=mesh, in_specs=in_specs, out_specs=out_specs, check_vma=False)
```

time: 1010 us -> 467 us (0.46)
  blocking collectives: 232 us -> 13.5 us
  matrix products: 244 us -> 74.5 us
  local copies, waits for them, and re-layouts: 131 us -> 39.1 us
  waiting for transfers between devices: 278 us -> 229 us
  Pallas kernels: 0 us -> 44.3 us
  other arithmetic: 72 us -> 28.1 us
  loops' own time: 10.6 us -> 0 us
    all_to_all x3 -> x0, waiting for transfers between devices: 196 us -> none  [the longest x1 137 us: shards(): lax.all_to_all(stacked, 'seq', split_axis=2, concat_axis=0, tiled=True)]
    all_to_all x1 -> x0, blocking collectives: 191 us -> none  [shards(): lax.all_to_all(head_grads, 'seq', split_axis=0, concat_axis=2, tiled=True)]
    dot_general x68 -> x14, matrix products: 244 us -> 74.5 us  [the longest x1 10.9 us: shards(): projected = jnp.dot(n1_wide, qkv_full, preferred_element_type=f32)]
    reduce_scatter x4 -> x3, waiting for transfers between devices: 39 us -> 133 us  [scatter_sum(): lax.psum_scatter(grad.astype(bf16), 'dp', scatter_dimension=0, tiled=True)]
    pallas_call x0 -> x2, Pallas kernels: none -> 44.3 us  [the longest x1 24.6 us: attention_back(): pl.pallas_call(attention_back_kernel, grid=(pairs,), in_specs=[column_spe...]
    psum x1, waiting for transfers between devices: 23.2 us -> 58.5 us  [scatter_sum(): return lax.psum(share, 'seq').astype(f32)]
    another operation x7 -> x0, local copies, waits for them, and re-layouts: 29.7 us -> none  [the longest x2 13.6 us: shards(): jnp.stack([query_grad.reshape(seq_total, D // seq_count), key_pad_grad[WI...]
    all_to_all x4 -> x0, local copies, waits for them, and re-layouts: 20.5 us -> none  [the longest x1 12.8 us: shards(): lax.all_to_all(head_grads, 'seq', split_axis=0, concat_axis=2, tiled=True)]
  transfers between devices with their start and end apart: 12 -> 13, of which waited for: 6 -> 7; matrix products, arithmetic and copies ran while one was open for 35% -> 20% of each run, Pallas kernels for 0% -> 4%
where the time goes in v1:
time: 467 us; the launch traced here: 458 us
  waiting for transfers between devices  229 us (49%)
  matrix products  74.5 us (16%)
  Pallas kernels  44.3 us (9%)
  local copies, waits for them, and re-layouts  39.1 us (8%)
  other arithmetic  28.1 us (6%)
  between operations  15.3 us (3%)
  starting transfers between devices  13.7 us (3%)
  blocking collectives  13.5 us (3%)
    reduce_scatter x3, waiting for transfers between devices, scatter_sum(): lax.psum_scatter(grad.astype(bf16), 'dp', scatter_dimension=0, tiled=True)  133 us
    psum x1, waiting for transfers between devices, scatter_sum(): return lax.psum(share, 'seq').astype(f32)  58.5 us
    unnamed x97, local copies, waits for them, and re-layouts  34.8 us
    all_gather x4, waiting for transfers between devices, gather(): return lax.all_gather(weight, 'dp', axis=0, tiled=True)  34.6 us
    pallas_call x1, Pallas kernels, attention_back(): pl.pallas_call(attention_back_kernel, grid=(pairs,), in_specs=[column_spe...  24.6 us
    pallas_call x1, Pallas kernels, attention(): pl.pallas_call(attention_kernel, grid=(pairs,), in_specs=[pl.BlockSpec(me...  19.7 us
    unnamed x1, blocking collectives  13.5 us
    dot_general x1, matrix products, shards(): projected = jnp.dot(n1_wide, qkv_full, preferred_element_type=f32)  10.9 us
  transfers between devices with their start and end apart: 13, of which 7 were waited for; matrix products, arithmetic and copies ran while one was open for 20% of the time, Pallas kernels for 4%

profile of v1, /device:TPU:0, one launch (start us, length us, event | category | flops | bytes accessed | tf_op | source)
XLA Modules:
  0.0 457.9 jit_solution(8330454294003479729)
XLA Ops:
  11.1 4.9 %collective-permute-start = (bf16[64,768]{1,0:T(8,128)(2,1)}, bf16[64,768]{1,0:T(8,128)(2,1)S(1)}, u32[]{:S(2)}, u32[]{:S(2)}) collective-permute-start(bf16[64,768]{1,0:T(8,128)(2,1)} %get-tuple-element.69), channel_id=1, source_target_pairs={{0,1},{1,2},{2,3},{4,5},{5,6},{6,7},{8,9},{9,10},{10,11},{12,13},{... | collective-permute-start | bytes 294920 | tf_op jit(solution)/shard_map/ppermute | solution.py:242
  21.8 13.5 %all-reduce.2 = (bf16[768]{0:T(1024)(128)(2,1)S(1)}, bf16[768]{0:T(1024)(128)(2,1)S(1)}) all-reduce(bf16[768]{0:T(1024)(128)(2,1)S(1)} %dynamic-update-slice, bf16[768]{0:T(1024)(128)(2,1)S(1)} %dynamic-update-slice.1), channel_id=1, replica_groups=mesh['dp'=8,'seq'=4] {'dp'}, use_global_device_ids=true, to_apply=%add | all-reduce | flops 1536 | bytes 6144
  36.9 3.2 fusion.38
  40.1 3.1 pad_maximum_fusion.5
  48.7 10.9 %fusion.47.q_ref.k_ref.v_ref = f32[1152,2304]{1,0:T(8,128)} fusion(bf16[1152,768]{1,0:T(8,128)(2,1)} %fusion.22, bf16[768,2304]{1,0:T(8,128)(2,1)} %all-gather.5.cloned.1.call-done), kind=kOutput, calls=%fused_computation.100 | convolution fusion | flops 4076863488 | bytes 15925248 | tf_op jit(solution)/shard_map/dot_general | solution.py:247
  59.6 19.7 %attention_forward.1 = (bf16[1024,768]{1,0:T(8,128)(2,1)S(1)}, bf16[6,8,256,256]{3,2,1,0:T(8,128)(2,1)S(1)}, bf16[1024,768]{1,0:T(8,128)(2,1)S(1)}, bf16[1152,768]{1,0:T(8,128)(2,1)S(1)}, bf16[1152,768]{1,0:T(8,128)(2,1)S(1)}) custom-call(s32[2]{0:T(128)S(1)} %pad_add_fusion.edge_ref, f32[1152,2304]{1,0:T(8,128)} %fusion.47.q_ref.k_ref.v_ref, ...), custom_call_target="tpu_custom_call" | custom-call | flops 805306368 | bytes 30000000 | tf_op jit(solution)/shard_map/attention_forward/pallas_call | solution.py:154
  85.6 3.9 fusion.46
  91.6 16.9 %all-gather.9.cloned.1.call-done = bf16[768,2304]{1,0:T(8,128)(2,1)} async-done(((bf16[96,2304]{1,0:T(8,128)(2,1)}), bf16[768,2304]{1,0:T(8,128)(2,1)}) %all-gather.9.cloned.1.call-update) | async-done | bytes 3538960 | tf_op jit(solution)/shard_map/all_gather | solution.py:220
  108.5 10.6 %fusion.42 = f32[1024,2304]{1,0:T(8,128)} fusion(bf16[768,2304]{1,0:T(8,128)(2,1)} %all-gather.9.cloned.1.call-done, f32[1024,768]{0,1:T(8,128)} %copy-done.19, f32[768]{0:T(1024)S(1)} %convert_element_type.109, f32[1024]{0:T(1024)S(1)} %add_rsqrt_fusion.2, f32[1024]{0:T(1024)S(1)} %broadcast_multiply_fusion.6), kind=kOutput, calls=%fused_computation.95 | convolution fusion | flops 3627024384 | bytes 16133120 | tf_op jit(solution)/shard_map/dot_general | solution.py:261
  119.1 17.7 %all-gather.11.cloned.1.call-done = bf16[1152,768]{1,0:T(8,128)(2,1)} async-done(((bf16[144,768]{1,0:T(8,128)(2,1)}), bf16[1152,768]{1,0:T(8,128)(2,1)}) %all-gather.11.cloned.1.call-update) | async-done | bytes 1769488 | tf_op jit(solution)/shard_map/all_gather | solution.py:220
  136.8 8.8 %fusion.5 = (bf16[1024,1152]{1,0:T(8,128)(2,1)S(1)}, bf16[1024,1152]{1,0:T(8,128)(2,1)S(1)}, bf16[1024,1152]{1,0:T(8,128)(2,1)}) fusion(f32[1024,2304]{1,0:T(8,128)} %fusion.42, bf16[1024,768]{1,0:T(8,128)(2,1)S(1)} %copy-done.29, bf16[1152,768]{1,0:T(8,128)(2,1)} %all-gather.11.cloned.1.call-done), kind=kOutput, calls=%fused_computation.10 | convolution fusion | flops 1830813696 | bytes 19857408 | tf_op jit(solution)/shard_map/td,fd->tf/dot_general | solution.py:271
  145.6 4.0 multiply_reduce_fusion.3
  154.6 24.6 %attention_backward.1 = (bf16[1024,768]{1,0:T(8,128)(2,1)S(1)}, bf16[1152,768]{1,0:T(8,128)(2,1)S(1)}, bf16[1152,768]{1,0:T(8,128)(2,1)S(1)}) custom-call(bf16[1024,768]{1,0:T(8,128)(2,1)S(1)} %convolution_convert_fusion.2.do_ref, bf16[1024,768]{1,0:T(8,128)(2,1)S(1)} %copy-done.8, bf16[1152,768]{1,0:T(8,128)(2,1)S(1)} %copy-done.4, ...), custom_call_target="tpu_custom_call" | custom-call | flops 1610612736 | bytes 20000000 | tf_op jit(solution)/shard_map/attention_backward/pallas_call | solution.py:193
  186.2 5.8 %copy.39 = bf16[768,2304]{1,0:T(8,128)(2,1)} copy(bf16[768,2304]{0,1:T(8,128)(2,1)} %pad_maximum_fusion.1) | data formatting | bytes 7077888
  193.5 4.4 convolution_convert_fusion.3
  198.1 5.7 %convolution_convert_fusion.1 = bf16[1152,768]{1,0:T(8,128)(2,1)} fusion(bf16[1024,1152]{1,0:T(8,128)(2,1)} %get-tuple-element.62, bf16[1024,768]{1,0:T(8,128)(2,1)} %param.15), kind=kOutput, calls=%fused_computation.36 | convolution fusion | flops 1812824064 | bytes 5701632 | tf_op jit(solution)/shard_map/tf,td->fd/dot_general | solution.py:269
  203.9 9.3 %convolution_convert_fusion = bf16[768,2304]{1,0:T(8,128)(2,1)} fusion(bf16[1024,1152]{1,0:T(8,128)(2,1)} %copy-done.41, bf16[1024,1152]{1,0:T(8,128)(2,1)} %copy-done.40, f32[1024,768]{0,1:T(8,128)} %copy-done.19, f32[768]{0:T(1024)S(1)} %convert_element_type.109, f32[1024]{0:T(1024)S(1)} %add_rsqrt_fusion.2, f32[1024]{0:T(1024)S(1)} %broadcast_multiply_fusion.6), kind=kOutput, calls=%fused_computation.1 | convolution fusion | flops 3638231040 | bytes 11414528 | tf_op jit(solution)/shard_map/td,tf->df/dot_general | solution.py:273
  223.3 5.5 %collective-permute-start.2 = (bf16[64,1536]{1,0:T(8,128)(2,1)S(1)}, bf16[64,1536]{1,0:T(8,128)(2,1)}, u32[]{:S(2)}, u32[]{:S(2)}) collective-permute-start(bf16[64,1536]{1,0:T(8,128)(2,1)S(1)} %pad_maximum_fusion.8), channel_id=1, source_target_pairs={{0,1},{1,2},{2,3},{4,5},{5,6},{6,7},{8,9},{9,10},{10,11},{12,13},{... | collective-permute-start | bytes 589832 | tf_op jit(solution)/shard_map/ppermute | solution.py:287
  228.8 3.6 add_convert_fusion
  242.4 37.8 %reduce-scatter.7.cloned.1.call-done = bf16[96,768]{1,0:T(8,128)(2,1)} async-done(((bf16[768,768]{1,0:T(8,128)(2,1)}), bf16[96,768]{1,0:T(8,128)(2,1)}) %reduce-scatter.7.cloned.1.call-update) | async-done | bytes 147472 | tf_op jit(solution)/shard_map/reduce_scatter | solution.py:224
  280.2 43.2 %reduce-scatter.11.cloned.1.call-done = bf16[144,768]{1,0:T(8,128)(2,1)} async-done(((bf16[1152,768]{1,0:T(8,128)(2,1)}), bf16[144,768]{1,0:T(8,128)(2,1)}) %reduce-scatter.11.cloned.1.call-update) | async-done | bytes 221200 | tf_op jit(solution)/shard_map/reduce_scatter | solution.py:224
  323.4 52.0 %reduce-scatter.9.cloned.1.call-done = bf16[96,2304]{1,0:T(8,128)(2,1)} async-done(((bf16[768,2304]{1,0:T(8,128)(2,1)}), bf16[96,2304]{1,0:T(8,128)(2,1)}) %reduce-scatter.9.cloned.1.call-update) | async-done | bytes 442384 | tf_op jit(solution)/shard_map/reduce_scatter | solution.py:224
  375.4 7.0 %multiply_reduce_fusion.2 = (f32[1024]{0:T(1024)S(1)}, f32[1024]{0:T(1024)S(1)}, f32[1024,768]{0,1:T(8,128)S(1)}) fusion(f32[768]{0:T(1024)S(1)} %convert_element_type.106, f32[1024]{0:T(1024)S(1)} %add_rsqrt_fusion.1, f32[1024]{0:T(1024)S(1)} %broadcast_multiply_fusion.3, bf16[1024,768]{0,1:T(8,128)(2,1)S(1)} %copy-done.14, ...), kind=kOutput, calls=%fused_computation.52 | convolution fusion | flops 3648256000 | bytes 12995584 | tf_op jit(solution)/shard_map/dot_general | solution.py:71
  385.1 58.5 %all-reduce.6.cloned.1.call-done = (bf16[96,2304]{0,1:T(8,128)(2,1)}, bf16[96,768]{1,0:T(8,128)(2,1)}, bf16[96,2304]{1,0:T(8,128)(2,1)}, bf16[144,768]{1,0:T(8,128)(2,1)}) async-done(((bf16[96,2304]{0,1:T(8,128)(2,1)}, bf16[96,768]{1,0:T(8,128)(2,1)}, bf16[96,2304]{1,0:T(8,128)(2,1)}, bf16[144,768]{1,0:T(8,128)(2,1)}), (bf16[96,2304]{0,1:T(8,128)(2,1)}, bf16[96,768]{1,0:T(8,128)(2,1)}, ...) | async-done | bytes 1253392 | tf_op jit(solution)/shard_map/psum | solution.py:225
  (166 shorter events, 68.0 us)
Async XLA Ops:
  7.2 12.9 %copy-start.38 = (u32[32]{0:T(128)S(1)}, u32[32]{0:T(128)}, u32[]{:S(2)}) copy-start(u32[32]{0:T(128)} %constant.55) | copy-start | bytes 388
  7.2 14.1 %copy-start.36 = (bf16[96]{0:T(256)(128)(2,1)S(1)}, bf16[96]{0:T(256)(128)(2,1)}, u32[]{:S(2)}) copy-start(bf16[96]{0:T(256)(128)(2,1)} %param.9) | copy-start | bytes 580
  7.2 14.3 %copy-start.35 = (bf16[96]{0:T(256)(128)(2,1)S(1)}, bf16[96]{0:T(256)(128)(2,1)}, u32[]{:S(2)}) copy-start(bf16[96]{0:T(256)(128)(2,1)} %param.12) | copy-start | bytes 580
  7.2 28.1 %copy-start.28 = (bf16[1024,768]{1,0:T(8,128)(2,1)S(1)}, bf16[1024,768]{1,0:T(8,128)(2,1)}, u32[]{:S(2)}) copy-start(bf16[1024,768]{1,0:T(8,128)(2,1)} %param.15) | copy-start | bytes 4718596
  7.2 41.5 %all-gather.5.cloned.1.call-start = ((), (), s32[]{:S(2)}) async-start(), calls=%async_computation.4 | async-start | bytes 3981312 | tf_op jit(solution)/shard_map/all_gather | solution.py:220
  7.9 77.6 %all-gather.7.cloned.1.call-start = ((), (), s32[]{:S(2)}) async-start(), calls=%async_computation.5 | async-start | bytes 1327104 | tf_op jit(solution)/shard_map/all_gather | solution.py:220
  8.7 99.8 %all-gather.9.cloned.1.call-start = ((), (), s32[]{:S(2)}) async-start(), calls=%async_computation.6 | async-start | bytes 3981312 | tf_op jit(solution)/shard_map/all_gather | solution.py:220
  9.4 127.4 %all-gather.11.cloned.1.call-start = ((), (), s32[]{:S(2)}) async-start(), calls=%async_computation.7 | async-start | bytes 1990656 | tf_op jit(solution)/shard_map/all_gather | solution.py:220
  11.1 32.3 %collective-permute-start = (bf16[64,768]{1,0:T(8,128)(2,1)}, bf16[64,768]{1,0:T(8,128)(2,1)S(1)}, u32[]{:S(2)}, u32[]{:S(2)}) collective-permute-start(bf16[64,768]{1,0:T(8,128)(2,1)} %get-tuple-element.69), channel_id=1, source_target_pairs={{0,1},{1,2},{2,3},{4,5},{5,6},{6,7},{8,9},{9,10},{10,11},{12,13},{... | collective-permute-start | bytes 294920 | tf_op jit(solution)/shard_map/ppermute | solution.py:242
  16.0 27.4 %collective-permute-start.1 = (bf16[64,768]{1,0:T(8,128)(2,1)}, bf16[64,768]{1,0:T(8,128)(2,1)}, u32[]{:S(2)}, u32[]{:S(2)}) collective-permute-start(bf16[64,768]{1,0:T(8,128)(2,1)} %get-tuple-element.70), channel_id=1, source_target_pairs={{1,0},{2,1},{3,2},{5,4},{6,5},{7,6},{9,8},{10,9},{11,10},{13,12},{... | collective-permute-start | bytes 294920 | tf_op jit(solution)/shard_map/ppermute | solution.py:243
  17.4 223.0 %reduce-scatter.13.cloned.1.call-start = ((), (), s32[]{:S(2)}) async-start(), calls=%async_computation.11 | async-start | bytes 3981312
  91.6 45.2 %copy-start.29 = (bf16[1024,768]{1,0:T(8,128)(2,1)S(1)}, bf16[1024,768]{1,0:T(8,128)(2,1)}, u32[]{:S(2)}) copy-start(bf16[1024,768]{1,0:T(8,128)(2,1)} %param.15) | copy-start | bytes 4718596
  154.6 24.7 %copy-start.27 = (bf16[1152,768]{1,0:T(8,128)(2,1)S(1)}, bf16[1152,768]{1,0:T(8,128)(2,1)}, u32[]{:S(2)}) copy-start(bf16[1152,768]{1,0:T(8,128)(2,1)} %fusion.22) | copy-start | bytes 5308420
  192.1 88.1 %reduce-scatter.7.cloned.1.call-start = ((), (), s32[]{:S(2)}) async-start(), calls=%async_computation.8 | async-start | bytes 1327104 | tf_op jit(solution)/shard_map/reduce_scatter | solution.py:224
  197.9 125.5 %reduce-scatter.11.cloned.1.call-start = ((), (), s32[]{:S(2)}) async-start(), calls=%async_computation.10 | async-start | bytes 1990656 | tf_op jit(solution)/shard_map/reduce_scatter | solution.py:224
  203.8 171.5 %reduce-scatter.9.cloned.1.call-start = ((), (), s32[]{:S(2)}) async-start(), calls=%async_computation.9 | async-start | bytes 3981312 | tf_op jit(solution)/shard_map/reduce_scatter | solution.py:224
  213.2 230.4 %all-reduce.6.cloned.1.call-start = ((), (), s32[]{:S(2)}) async-start(), calls=%async_computation.12 | async-start | bytes 2801664 | tf_op jit(solution)/shard_map/psum | solution.py:225
  219.2 9.7 %copy-start.33 = (bf16[1152,768]{1,0:T(8,128)(2,1)S(1)}, bf16[1152,768]{1,0:T(8,128)(2,1)}, u32[]{:S(2)}) copy-start(bf16[1152,768]{1,0:T(8,128)(2,1)} %all-gather.11.cloned.1.call-done) | copy-start | bytes 5308420
  221.9 15.1 %collective-permute-start.3 = (bf16[64,1536]{1,0:T(8,128)(2,1)S(1)}, bf16[64,1536]{1,0:T(8,128)(2,1)}, u32[]{:S(2)}, u32[]{:S(2)}) collective-permute-start(bf16[64,1536]{1,0:T(8,128)(2,1)S(1)} %pad_maximum_fusion.9), channel_id=1, source_target_pairs={{1,0},{2,1},{3,2},{5,4},{6,5},{7,6},{9,8},{10,9},{11,10},{13,12},{... | collective-permute-start | bytes 589832 | tf_op jit(solution)/shard_map/ppermute | solution.py:286
  223.3 13.6 %collective-permute-start.2 = (bf16[64,1536]{1,0:T(8,128)(2,1)S(1)}, bf16[64,1536]{1,0:T(8,128)(2,1)}, u32[]{:S(2)}, u32[]{:S(2)}) collective-permute-start(bf16[64,1536]{1,0:T(8,128)(2,1)S(1)} %pad_maximum_fusion.8), channel_id=1, source_target_pairs={{0,1},{1,2},{2,3},{4,5},{5,6},{6,7},{8,9},{9,10},{10,11},{12,13},{... | collective-permute-start | bytes 589832 | tf_op jit(solution)/shard_map/ppermute | solution.py:287
  237.0 138.4 %copy-start.10 = (bf16[1024,768]{1,0:T(8,128)(2,1)S(1)}, bf16[1024,768]{1,0:T(8,128)(2,1)}, u32[]{:S(2)}) copy-start(bf16[1024,768]{1,0:T(8,128)(2,1)} %copy-done.9) | copy-start | bytes 4718596
  237.0 138.4 %copy-start.14 = (bf16[1024,768]{0,1:T(8,128)(2,1)S(1)}, bf16[1024,768]{0,1:T(8,128)(2,1)}, u32[]{:S(2)}) copy-start(bf16[1024,768]{0,1:T(8,128)(2,1)} %copy.30) | copy-start | bytes 4718596
  383.5 66.7 %copy-start.25 = (bf16[96,2304]{0,1:T(8,128)(2,1)S(1)}, bf16[96,2304]{0,1:T(8,128)(2,1)}, u32[]{:S(2)}) copy-start(bf16[96,2304]{0,1:T(8,128)(2,1)} %copy.34) | copy-start | bytes 1327108
  385.1 65.5 %copy-start.37 = (bf16[96]{0:T(256)(128)(2,1)S(1)}, bf16[96]{0:T(256)(128)(2,1)}, u32[]{:S(2)}) copy-start(bf16[96]{0:T(256)(128)(2,1)} %param.9) | copy-start | bytes 580
  (31 other events, 126.1 us)
Sparse Core Ops, SparseCore 0:
  9.9 36.6 all-gather.4
  48.5 24.0 all-gather.6
  74.5 33.9 all-gather.8
  110.2 26.5 all-gather.10
  192.2 48.0 reduce-scatter.12
  243.4 36.7 reduce-scatter.6
  283.9 39.3 reduce-scatter.10
  327.2 48.0 reduce-scatter.8
  378.8 64.8 all-reduce.5
